TPU v7x, 256 devices: a whole 4x4x8 slice. The times are simulated.
256 devices in a mesh: dp: 8 (over z_lo, core), seq: 32 (over y, x, z_hi).
Axes of the slice: x: 4, y: 4, z: 8 (z_hi: 2, z_lo: 4; z = z_hi * 4 + z_lo), core: 2. Of those that a mesh axis runs over, the one named last changes fastest.
Arguments:
- first_input: bfloat16 [8, 16384, 128], P('dp', 'seq'), may hold values from -6 to 6
- value_input: bfloat16 [8, 16384, 128], P('dp', 'seq'), may hold values from -6 to 6
- gate_input: bfloat16 [8, 16384, 128], P('dp', 'seq'), may hold values from -6 to 6
- cotangent: bfloat16 [8, 16384, 128], P('dp', 'seq'), may hold values from -6 to 6
- filter_taps: float32 [16384, 128], P('seq'), may hold values from -4 to 4
- skip_weight: float32 [128], replicated, may hold values from -4 to 4
Outputs:
- layer_output: bfloat16 [8, 16384, 128], P('dp', 'seq')
- filter_grad: float32 [16384, 128], P('seq')
All inputs are finite; a program needn't handle non-finite values.
Results may differ from a plain program's by a relative error of at most 0.001.
Values sent between devices are 32-bit elements; how exact they have to be, the bound alone decides.
A program may use at most 64 MiB of HBM per device.

v0:
```python
import functools
import math
import jax
import jax.numpy as jnp
from jax import lax
from jax.sharding import PartitionSpec as P


def angles(numer, period):
    return 2.0 * math.pi / period * (numer % period).astype(jnp.float32)


def rotate(real_part, imag_part, phase, direction):
    cosine = jnp.cos(phase)
    sine = direction * jnp.sin(phase)
    return (real_part * cosine - imag_part * sine, real_part * sine + imag_part * cosine)


def local_transform(real_part, imag_part, direction):
    count, length = real_part.shape
    outer = 1 << (length.bit_length() - 1) // 2
    inner = length // outer
    real_cube = real_part.reshape(count, outer, inner)
    imag_cube = imag_part.reshape(count, outer, inner)
    outer_idx = lax.iota(jnp.int32, outer)
    inner_idx = lax.iota(jnp.int32, inner)
    first_phase = angles(outer_idx[:, None] * outer_idx[None, :], outer)
    first_cos = jnp.cos(first_phase)
    first_sin = direction * jnp.sin(first_phase)
    mix = functools.partial(
        jnp.einsum, precision=lax.Precision.HIGHEST, preferred_element_type=jnp.float32
    )
    section_real = mix("kp,cpq->ckq", first_cos, real_cube) - mix(
        "kp,cpq->ckq", first_sin, imag_cube
    )
    section_imag = mix("kp,cpq->ckq", first_cos, imag_cube) + mix(
        "kp,cpq->ckq", first_sin, real_cube
    )
    twiddle = angles(outer_idx[:, None] * inner_idx[None, :], length)
    section_real, section_imag = rotate(section_real, section_imag, twiddle, direction)
    second_phase = angles(inner_idx[:, None] * inner_idx[None, :], inner)
    second_cos = jnp.cos(second_phase)
    second_sin = direction * jnp.sin(second_phase)
    final_real = mix("ckq,jq->ckj", section_real, second_cos) - mix(
        "ckq,jq->ckj", section_imag, second_sin
    )
    final_imag = mix("ckq,jq->ckj", section_imag, second_cos) + mix(
        "ckq,jq->ckj", section_real, second_sin
    )
    final_real = jnp.transpose(final_real, (0, 2, 1)).reshape(count, length)
    final_imag = jnp.transpose(final_imag, (0, 2, 1)).reshape(count, length)
    return (final_real, final_imag)


def channel_layout(gated, weighted, filter_taps, gate_input, skip_weight):
    batch_local = gated.shape[0]
    moved_gated, moved_weighted, moved_taps = (
        lax.all_to_all(gated, "seq", split_axis=2, concat_axis=1, tiled=True),
        lax.all_to_all(weighted, "seq", split_axis=2, concat_axis=1, tiled=True),
        lax.all_to_all(filter_taps[None], "seq", split_axis=2, concat_axis=1, tiled=True),
    )
    length = moved_gated.shape[1]
    narrow = moved_gated.shape[2]
    spread = batch_local * narrow
    gated_rows = jnp.transpose(moved_gated, (0, 2, 1)).reshape(spread, length)
    weighted_rows = jnp.transpose(moved_weighted, (0, 2, 1)).reshape(spread, length)
    taps_rows = jnp.transpose(moved_taps[0], (1, 0))
    rows_all = jnp.concatenate([gated_rows, taps_rows, weighted_rows], axis=0)
    count = rows_all.shape[0]
    twist = angles(lax.iota(jnp.int32, length), 2 * length)[None, :]
    cos_twist = jnp.cos(twist)
    sin_twist = jnp.sin(twist)
    real_in = jnp.concatenate([rows_all, rows_all * cos_twist], axis=0)
    imag_in = jnp.concatenate([jnp.zeros_like(rows_all), -rows_all * sin_twist], axis=0)
    spec_real, spec_imag = local_transform(real_in, imag_in, -1.0)
    spec_real = spec_real.reshape(2, count, length)
    spec_imag = spec_imag.reshape(2, count, length)
    gated_real = spec_real[:, :spread].reshape(2, batch_local, narrow, length)
    gated_imag = spec_imag[:, :spread].reshape(2, batch_local, narrow, length)
    taps_real = spec_real[:, spread : spread + narrow][:, None]
    taps_imag = spec_imag[:, spread : spread + narrow][:, None]
    source_real = spec_real[:, spread + narrow :].reshape(2, batch_local, narrow, length)
    source_imag = spec_imag[:, spread + narrow :].reshape(2, batch_local, narrow, length)
    conv_real = (gated_real * taps_real - gated_imag * taps_imag).reshape(2, spread, length)
    conv_imag = (gated_real * taps_imag + gated_imag * taps_real).reshape(2, spread, length)
    grad_real = jnp.sum(source_real * gated_real + source_imag * gated_imag, axis=1)
    grad_imag = jnp.sum(source_imag * gated_real - source_real * gated_imag, axis=1)
    back_real = jnp.concatenate([conv_real, grad_real], axis=1).reshape(-1, length)
    back_imag = jnp.concatenate([conv_imag, grad_imag], axis=1).reshape(-1, length)
    back_real, back_imag = local_transform(back_real, back_imag, 1.0)
    back_real = back_real.reshape(2, -1, length)
    back_imag = back_imag.reshape(2, -1, length)
    joined = (back_real[0] + back_real[1] * cos_twist - back_imag[1] * sin_twist) / (2.0 * length)
    convolved = jnp.transpose(joined[:spread].reshape(batch_local, narrow, length), (0, 2, 1))
    grad_time = lax.psum(jnp.transpose(joined[spread:], (1, 0)), "dp")
    convolved, grad_back = (
        lax.all_to_all(convolved, "seq", split_axis=1, concat_axis=2, tiled=True),
        lax.all_to_all(grad_time[None], "seq", split_axis=1, concat_axis=2, tiled=True),
    )
    layer_output = (gate_input.astype(jnp.float32) * (convolved + skip_weight * gated)).astype(
        jnp.bfloat16
    )
    scale = 1.0 / math.sqrt(batch_local * lax.axis_size("dp") * length)
    return (layer_output, grad_back[0] * scale)


def shards(first_input, value_input, gate_input, cotangent, filter_taps, skip_weight):
    gated = first_input.astype(jnp.float32) * value_input.astype(jnp.float32)
    weighted = cotangent.astype(jnp.float32) * gate_input.astype(jnp.float32)
    return channel_layout(gated, weighted, filter_taps, gate_input, skip_weight)


def solution(mesh):
    placed = (
        P("dp", "seq", None),
        P("dp", "seq", None),
        P("dp", "seq", None),
        P("dp", "seq", None),
        P("seq", None),
        P(),
    )
    return jax.shard_map(
        shards,
        mesh=mesh,
        in_specs=placed,
        out_specs=(P("dp", "seq", None), P("seq", None)),
        check_vma=False,
    )
```

profile of v0, /device:TPU:2, one launch (start us, length us, event | category | flops | bytes accessed | tf_op | source)
XLA Modules:
  0.0 486.5 jit_solution(10669566144408117033)
XLA Ops:
  7.2 1.1 convert_multiply_fusion.1
  8.3 0.8 copy.157
  9.1 14.2 %all-to-all-start.2 = ((f32[1,512,128]{1,0,2:T(1,128)}), f32[1,512,128]{1,0,2:T(1,128)S(1)}, u32[]{:S(2)}, u32[]{:S(2)}) async-start(f32[1,512,128]{1,0,2:T(1,128)} %copy.157), calls=%async_computation.2 | async-start | bytes 524288 | tf_op jit(solution)/shard_map/all_to_all | solution.py:59
  24.2 11.4 %all-to-all-done.2 = f32[1,512,128]{1,0,2:T(1,128)S(1)} async-done(((f32[1,512,128]{1,0,2:T(1,128)}), f32[1,512,128]{1,0,2:T(1,128)S(1)}, u32[]{:S(2)}, u32[]{:S(2)}) %all-to-all-start.2) | async-done | bytes 262176 | tf_op jit(solution)/shard_map/all_to_all | solution.py:59
  35.6 5.0 %all-to-all-start.1 = ((f32[1,512,128]{1,0,2:T(1,128)}), f32[1,512,128]{1,0,2:T(1,128)S(1)}, u32[]{:S(2)}, u32[]{:S(2)}) async-start(f32[1,512,128]{1,0,2:T(1,128)} %copy.211), calls=%async_computation.1 | async-start | bytes 524288 | tf_op jit(solution)/shard_map/all_to_all | solution.py:60
  40.6 0.8 copy.153
  42.2 10.6 %all-to-all-done.1 = f32[1,512,128]{1,0,2:T(1,128)S(1)} async-done(((f32[1,512,128]{1,0,2:T(1,128)}), f32[1,512,128]{1,0,2:T(1,128)S(1)}, u32[]{:S(2)}, u32[]{:S(2)}) %all-to-all-start.1) | async-done | bytes 262176 | tf_op jit(solution)/shard_map/all_to_all | solution.py:60
  52.9 6.1 %all-to-all-start = ((f32[1,512,128]{1,0,2:T(1,128)}), f32[1,512,128]{1,0,2:T(1,128)S(1)}, u32[]{:S(2)}, u32[]{:S(2)}) async-start(f32[1,512,128]{1,0,2:T(1,128)} %copy.153), calls=%async_computation | async-start | bytes 524288 | tf_op jit(solution)/shard_map/all_to_all | solution.py:58
  60.5 0.9 fusion.50
  62.3 8.7 %all-to-all-done = f32[1,512,128]{1,0,2:T(1,128)S(1)} async-done(((f32[1,512,128]{1,0,2:T(1,128)}), f32[1,512,128]{1,0,2:T(1,128)S(1)}, u32[]{:S(2)}, u32[]{:S(2)}) %all-to-all-start) | async-done | bytes 262176 | tf_op jit(solution)/shard_map/all_to_all | solution.py:58
  72.1 1.7 fusion.7
  73.8 2.8 fusion.45
  76.6 2.8 convolution_subtract_fusion
  79.5 1.7 convolution_add_fusion
  81.1 3.4 fusion.11
  84.5 4.0 fusion.15
  88.5 4.0 add_bitcast_fusion
  92.5 3.0 copy.175
  95.6 3.1 reshape_reshape.15
  98.6 5.4 %subtract_bitcast_fusion = f32[24,128,128]{1,2,0:T(8,128)} fusion(f32[24,128,128]{2,1,0:T(8,128)} %fusion.15, f32[24,128,128]{2,1,0:T(8,128)S(1)} %convolution_add_fusion, f32[24,128,128]{2,1,0:T(8,128)S(1)} %convolution_subtract_fusion, f32[128,128]{0,1:T(8,128)S(1)} %copy.169, f32[128,128]{0,1:T(8,128)S(1)} %copy.167), kind=kOutput, calls=%fused_computation.8 | convolution fusion | flops 605798400 | bytes 6422528 | tf_op jit(solution)/shard_map/ckq,jq->ckj/dot_general | solution.py:44
  104.0 3.2 copy.172
  107.2 3.2 reshape_reshape.14
  110.4 2.4 multiply_subtract_fusion.2
  113.5 1.9 fusion.41
  115.7 1.9 fusion.39
  117.6 1.9 fusion.5
  119.5 1.9 fusion.4
  121.5 2.0 fusion.18
  123.5 2.2 fusion.17
  125.7 2.0 fusion.2
  128.5 2.0 copy.188
  130.6 2.0 fusion.3
  133.7 0.9 fusion.9
  135.5 12.0 %copy.189 = f32[1,16384,4]{2,0,1:T(1,128)} copy(f32[1,16384,4]{1,2,0:T(4,128)S(1)} %get-tuple-element.17) | data formatting | bytes 524288 | tf_op jit(solution)/shard_map/transpose | solution.py:94
  148.0 74.5 %reduce = f32[16384,4]{1,0:T(8,128)} reduce(f32[16384,1,4]{2,1,0:T(1,128)} %bitcast.179, f32[]{:T(128)} %broadcast.236), dimensions={1}, to_apply=%bitcast.163.reduce_sub_computation | reduce | bytes 524292
  222.6 9.5 %reshape.143 = f32[32,1,2048]{2,1,0:T(1,128)} reshape(f32[16384,4]{1,0:T(8,128)} %reduce) | data formatting | bytes 524288
  232.0 5.9 %all-to-all-start.3 = ((f32[32,1,2048]{2,1,0:T(1,128)}), f32[32,1,2048]{2,1,0:T(1,128)S(1)}, u32[]{:S(2)}, u32[]{:S(2)}) async-start(f32[32,1,2048]{2,1,0:T(1,128)} %reshape.143), calls=%async_computation.3 | async-start | bytes 524288 | tf_op jit(solution)/shard_map/all_to_all | solution.py:97
  238.7 77.0 %all-reduce.3.cloned.1.call-done = f32[1,16384,4]{1,2,0:T(4,128)} async-done(((f32[1,16384,4]{1,2,0:T(4,128)}), f32[1,16384,4]{1,2,0:T(4,128)}) %all-reduce.3.cloned.1.call-update) | async-done | bytes 262160 | tf_op jit(solution)/shard_map/psum | solution.py:95
  315.7 14.8 %copy.193 = f32[1,16384,4]{2,0,1:T(1,128)} copy(f32[1,16384,4]{1,2,0:T(4,128)} %all-reduce.3.cloned.1.call-done) | data formatting | bytes 524288 | tf_op jit(solution)/shard_map/psum | solution.py:95
  330.6 74.5 %reduce.2 = f32[16384,4]{1,0:T(8,128)} reduce(f32[16384,1,4]{2,1,0:T(1,128)} %bitcast.180, f32[]{:T(128)} %broadcast.236), dimensions={1}, to_apply=%bitcast.165.reduce_sub_computation | reduce | bytes 524292
  405.1 9.1 %reshape.145 = f32[32,1,2048]{2,1,0:T(1,128)} reshape(f32[16384,4]{1,0:T(8,128)} %reduce.2) | data formatting | bytes 524288
  414.2 10.4 %all-to-all-start.4 = ((f32[32,1,2048]{2,1,0:T(1,128)}), f32[32,1,2048]{2,1,0:T(1,128)S(1)}, u32[]{:S(2)}, u32[]{:S(2)}) async-start(f32[32,1,2048]{2,1,0:T(1,128)} %reshape.145), calls=%async_computation.4 | async-start | bytes 524288 | tf_op jit(solution)/shard_map/all_to_all | solution.py:98
  424.6 1.3 reduce.1
  425.9 14.8 %reshape.144 = f32[16384,1,4]{2,1,0:T(1,128)} reshape(f32[32,2048]{1,0:T(8,128)S(1)} %reduce.1) | data formatting | bytes 524288
  440.6 5.3 %copy.212 = f32[1,32,512,4]{2,1,3,0:T(8,128)S(1)} copy(f32[1,32,512,4]{3,2,1,0:T(8,128)} %bitcast.181) | data formatting | bytes 524288 | tf_op jit(solution)/shard_map/all_to_all | solution.py:97
  447.1 1.3 reduce.3
  448.4 14.8 %reshape.146 = f32[16384,1,4]{2,1,0:T(1,128)} reshape(f32[32,2048]{1,0:T(8,128)S(1)} %reduce.3) | data formatting | bytes 524288
  463.2 15.0 %copy.194 = f32[1,16384,4]{1,2,0:T(4,128)S(1)} copy(f32[1,16384,4]{2,0,1:T(1,128)} %bitcast.182) | data formatting | bytes 524288 | tf_op jit(solution)/shard_map/all_to_all | solution.py:98
  (82 shorter events, 12.4 us)
Async XLA Ops:
  7.2 16.2 %copy-start.15 = (f32[512,128]{1,0:T(8,128)S(1)}, f32[512,128]{1,0:T(8,128)}, u32[]{:S(2)}) copy-start(f32[512,128]{1,0:T(8,128)} %param.10) | copy-start | bytes 786436
  7.2 33.4 %copy-start.10 = (bf16[1,512,128]{2,1,0:T(8,128)(2,1)S(1)}, bf16[1,512,128]{2,1,0:T(8,128)(2,1)}, u32[]{:S(2)}) copy-start(bf16[1,512,128]{2,1,0:T(8,128)(2,1)} %param.7) | copy-start | bytes 393220
  7.2 33.4 %copy-start.12 = (bf16[1,512,128]{2,1,0:T(8,128)(2,1)S(1)}, bf16[1,512,128]{2,1,0:T(8,128)(2,1)}, u32[]{:S(2)}) copy-start(bf16[1,512,128]{2,1,0:T(8,128)(2,1)} %param.6) | copy-start | bytes 393220
  9.1 26.5 %all-to-all-start.2 = ((f32[1,512,128]{1,0,2:T(1,128)}), f32[1,512,128]{1,0,2:T(1,128)S(1)}, u32[]{:S(2)}, u32[]{:S(2)}) async-start(f32[1,512,128]{1,0,2:T(1,128)} %copy.157), calls=%async_computation.2 | async-start | bytes 524288 | tf_op jit(solution)/shard_map/all_to_all | solution.py:59
  35.6 17.3 %all-to-all-start.1 = ((f32[1,512,128]{1,0,2:T(1,128)}), f32[1,512,128]{1,0,2:T(1,128)S(1)}, u32[]{:S(2)}, u32[]{:S(2)}) async-start(f32[1,512,128]{1,0,2:T(1,128)} %copy.211), calls=%async_computation.1 | async-start | bytes 524288 | tf_op jit(solution)/shard_map/all_to_all | solution.py:60
  52.9 18.1 %all-to-all-start = ((f32[1,512,128]{1,0,2:T(1,128)}), f32[1,512,128]{1,0,2:T(1,128)S(1)}, u32[]{:S(2)}, u32[]{:S(2)}) async-start(f32[1,512,128]{1,0,2:T(1,128)} %copy.153), calls=%async_computation | async-start | bytes 524288 | tf_op jit(solution)/shard_map/all_to_all | solution.py:58
  60.5 10.9 %copy-start.7 = (f32[16384]{0:T(1024)}, f32[16384]{0:T(1024)S(1)}, u32[]{:S(2)}) copy-start(f32[16384]{0:T(1024)S(1)} %fusion.51) | copy-start | bytes 196612
  62.3 9.8 %copy-start.1 = (f32[4,128,128]{1,2,0:T(8,128)}, f32[4,128,128]{1,2,0:T(8,128)S(1)}, u32[]{:S(2)}) copy-start(f32[4,128,128]{1,2,0:T(8,128)S(1)} %copy.164) | copy-start | bytes 786436
  71.4 0.7 copy-start.3
  76.6 2.9 copy-start.2
  76.6 2.9 copy-start.4
  107.2 3.2 copy-start
  119.5 1.9 copy-start.6
  132.7 1.0 copy-start.5
  132.7 1.0 copy-start.8
  132.7 1.0 copy-start.14
  232.0 182.2 %all-to-all-start.3 = ((f32[32,1,2048]{2,1,0:T(1,128)}), f32[32,1,2048]{2,1,0:T(1,128)S(1)}, u32[]{:S(2)}, u32[]{:S(2)}) async-start(f32[32,1,2048]{2,1,0:T(1,128)} %reshape.143), calls=%async_computation.3 | async-start | bytes 524288 | tf_op jit(solution)/shard_map/all_to_all | solution.py:97
  238.0 77.8 %all-reduce.3.cloned.1.call-start = ((), (), s32[]{:S(2)}) async-start(), calls=%async_computation.5 | async-start | bytes 524288 | tf_op jit(solution)/shard_map/psum | solution.py:95
  414.2 33.0 %all-to-all-start.4 = ((f32[32,1,2048]{2,1,0:T(1,128)}), f32[32,1,2048]{2,1,0:T(1,128)S(1)}, u32[]{:S(2)}, u32[]{:S(2)}) async-start(f32[32,1,2048]{2,1,0:T(1,128)} %reshape.145), calls=%async_computation.4 | async-start | bytes 524288 | tf_op jit(solution)/shard_map/all_to_all | solution.py:98
  440.6 5.7 %copy-start.9 = (bf16[1,512,128]{2,1,0:T(8,128)(2,1)S(1)}, bf16[1,512,128]{2,1,0:T(8,128)(2,1)}, u32[]{:S(2)}) copy-start(bf16[1,512,128]{2,1,0:T(8,128)(2,1)} %param.8) | copy-start | bytes 393220
  440.6 5.7 %copy-start.11 = (bf16[1,512,128]{2,1,0:T(8,128)(2,1)S(1)}, bf16[1,512,128]{2,1,0:T(8,128)(2,1)}, u32[]{:S(2)}) copy-start(bf16[1,512,128]{2,1,0:T(8,128)(2,1)} %param.7) | copy-start | bytes 393220
  440.6 5.7 %copy-start.13 = (bf16[1,512,128]{2,1,0:T(8,128)(2,1)S(1)}, bf16[1,512,128]{2,1,0:T(8,128)(2,1)}, u32[]{:S(2)}) copy-start(bf16[1,512,128]{2,1,0:T(8,128)(2,1)} %param.6) | copy-start | bytes 393220
  440.6 5.7 %copy-start.16 = (f32[128]{0:T(128)S(1)}, f32[128]{0:T(128)}, u32[]{:S(2)}) copy-start(f32[128]{0:T(128)} %param.11) | copy-start | bytes 1540
Sparse Core Ops, SparseCore 0:
  242.0 73.7 all-reduce.2
where the time goes:
time: 491 us; the launch traced here: 486 us
  other arithmetic  160 us (33%)
  local copies, waits for them, and re-layouts  120 us (24%)
  waiting for transfers between devices  108 us (22%)
  starting transfers between devices  41.7 us (8%)
  matrix products  41.6 us (8%)
  between operations  14.9 us (3%)
    unnamed x3, other arithmetic  149 us
    psum x1, waiting for transfers between devices, channel_layout(): grad_time = lax.psum(jnp.transpose(joined[spread:], (1, 0)), 'dp')  77 us
    unnamed x49, local copies, waits for them, and re-layouts  51.3 us
    all_to_all x1, local copies, waits for them, and re-layouts, channel_layout(): lax.all_to_all(grad_time[None], 'seq', split_axis=1, concat_axis=2, tiled...  15 us
    psum x1, local copies, waits for them, and re-layouts, channel_layout(): grad_time = lax.psum(jnp.transpose(joined[spread:], (1, 0)), 'dp')  14.8 us
    all_to_all x1, starting transfers between devices, channel_layout(): lax.all_to_all(weighted, 'seq', split_axis=2, concat_axis=1, tiled=True)  14.2 us
    transpose x1, local copies, waits for them, and re-layouts, channel_layout(): jnp.transpose(joined[:spread].reshape(batch_local, narrow, length), (0, 2...  12 us
    all_to_all x1, waiting for transfers between devices, channel_layout(): lax.all_to_all(weighted, 'seq', split_axis=2, concat_axis=1, tiled=True)  11.4 us
  transfers between devices with their start and end apart: 6, of which 4 were waited for; matrix products, arithmetic and copies ran while one was open for 26% of the time, Pallas kernels for 0%

commit v1 on v0

--- a/solution.py
+++ b/solution.py
@@ -55,7 +55,10 @@
 def channel_layout(gated, weighted, filter_taps, gate_input, skip_weight):
     batch_local = gated.shape[0]
     moved_gated, moved_weighted, moved_taps = (
-        lax.all_to_all(gated, "seq", split_axis=2, concat_axis=1, tiled=True),
+        jnp.concatenate(
+            lax.all_to_all(jnp.stack(jnp.split(gated, lax.axis_size("seq"), axis=2)), "seq", 0, 0),
+            axis=1,
+        ),
         lax.all_to_all(weighted, "seq", split_axis=2, concat_axis=1, tiled=True),
         lax.all_to_all(filter_taps[None], "seq", split_axis=2, concat_axis=1, tiled=True),
     )

time: 491 us -> 495 us (level)
    all_to_all x1, starting transfers between devices: 14.2 us -> 4.98 us  [channel_layout(): lax.all_to_all(weighted, 'seq', split_axis=2, concat_axis=1, tiled=True)]
    all_to_all x1, starting transfers between devices: 6.13 us -> 14.2 us  [channel_layout(): lax.all_to_all(jnp.stack(jnp.split(gated, lax.axis_size('seq'), axis=2)),...]
    unnamed x49 -> x56, local copies, waits for them, and re-layouts: 51.3 us -> 55.1 us
where the time goes in v1:
time: 495 us; the launch traced here: 489 us
  other arithmetic  160 us (32%)
  local copies, waits for them, and re-layouts  123 us (25%)
  waiting for transfers between devices  108 us (22%)
  starting transfers between devices  42 us (8%)
  matrix products  41.4 us (8%)
  between operations  14.9 us (3%)
    unnamed x3, other arithmetic  149 us
    psum x1, waiting for transfers between devices, channel_layout(): grad_time = lax.psum(jnp.transpose(joined[spread:], (1, 0)), 'dp')  77 us
    unnamed x56, local copies, waits for them, and re-layouts  55.1 us
    all_to_all x1, local copies, waits for them, and re-layouts, channel_layout(): lax.all_to_all(grad_time[None], 'seq', split_axis=1, concat_axis=2, tiled...  15 us
    psum x1, local copies, waits for them, and re-layouts, channel_layout(): grad_time = lax.psum(jnp.transpose(joined[spread:], (1, 0)), 'dp')  14.8 us
    all_to_all x1, starting transfers between devices, channel_layout(): lax.all_to_all(jnp.stack(jnp.split(gated, lax.axis_size('seq'), axis=2)),...  14.2 us
    transpose x1, local copies, waits for them, and re-layouts, channel_layout(): jnp.transpose(joined[:spread].reshape(batch_local, narrow, length), (0, 2...  12 us
    all_to_all x1, waiting for transfers between devices, channel_layout(): lax.all_to_all(weighted, 'seq', split_axis=2, concat_axis=1, tiled=True)  10.7 us
  transfers between devices with their start and end apart: 6, of which 4 were waited for; matrix products, arithmetic and copies ran while one was open for 26% of the time, Pallas kernels for 0%

profile of v1, /device:TPU:2, one launch (start us, length us, event | category | flops | bytes accessed | tf_op | source)
XLA Modules:
  0.0 489.1 jit_solution(3527387899514724409)
XLA Ops:
  7.2 1.1 copy.151
  8.3 1.1 copy.152
  11.9 14.2 %all-to-all-start = ((f32[32,1,512,4]{2,3,1,0:T(4,128)}), f32[32,1,512,4]{2,3,1,0:T(4,128)S(1)}, u32[]{:S(2)}, u32[]{:S(2)}) async-start(f32[32,1,512,4]{2,3,1,0:T(4,128)} %copy.153), calls=%async_computation | async-start | bytes 524288 | tf_op jit(solution)/shard_map/all_to_all | solution.py:59
  26.5 1.1 convert_multiply_fusion
  27.7 10.7 %all-to-all-done = f32[32,1,512,4]{2,3,1,0:T(4,128)S(1)} async-done(((f32[32,1,512,4]{2,3,1,0:T(4,128)}), f32[32,1,512,4]{2,3,1,0:T(4,128)S(1)}, u32[]{:S(2)}, u32[]{:S(2)}) %all-to-all-start) | async-done | bytes 262176 | tf_op jit(solution)/shard_map/all_to_all | solution.py:59
  38.3 5.0 %all-to-all-start.2 = ((f32[1,512,128]{1,0,2:T(1,128)}), f32[1,512,128]{1,0,2:T(1,128)S(1)}, u32[]{:S(2)}, u32[]{:S(2)}) async-start(f32[1,512,128]{1,0,2:T(1,128)} %convert_multiply_fusion), calls=%async_computation.2 | async-start | bytes 524288 | tf_op jit(solution)/shard_map/all_to_all | solution.py:62
  44.9 10.7 %all-to-all-done.2 = f32[1,512,128]{1,0,2:T(1,128)S(1)} async-done(((f32[1,512,128]{1,0,2:T(1,128)}), f32[1,512,128]{1,0,2:T(1,128)S(1)}, u32[]{:S(2)}, u32[]{:S(2)}) %all-to-all-start.2) | async-done | bytes 262176 | tf_op jit(solution)/shard_map/all_to_all | solution.py:62
  55.6 6.3 %all-to-all-start.1 = ((f32[1,512,128]{1,0,2:T(1,128)}), f32[1,512,128]{1,0,2:T(1,128)S(1)}, u32[]{:S(2)}, u32[]{:S(2)}) async-start(f32[1,512,128]{1,0,2:T(1,128)} %copy.211), calls=%async_computation.1 | async-start | bytes 524288 | tf_op jit(solution)/shard_map/all_to_all | solution.py:63
  63.5 0.9 fusion.51
  65.0 8.7 %all-to-all-done.1 = f32[1,512,128]{1,0,2:T(1,128)S(1)} async-done(((f32[1,512,128]{1,0,2:T(1,128)}), f32[1,512,128]{1,0,2:T(1,128)S(1)}, u32[]{:S(2)}, u32[]{:S(2)}) %all-to-all-start.1) | async-done | bytes 262176 | tf_op jit(solution)/shard_map/all_to_all | solution.py:63
  74.9 1.7 fusion.7
  76.6 2.8 fusion.46
  79.4 2.8 convolution_subtract_fusion
  82.2 1.7 convolution_add_fusion
  83.9 3.0 fusion.11
  86.9 4.0 fusion.15
  90.9 4.0 add_bitcast_fusion
  94.9 3.0 copy.175
  97.9 3.0 reshape_reshape.15
  101.0 5.4 %subtract_bitcast_fusion = f32[24,128,128]{1,2,0:T(8,128)} fusion(f32[24,128,128]{2,1,0:T(8,128)} %fusion.15, f32[24,128,128]{2,1,0:T(8,128)S(1)} %convolution_add_fusion, f32[24,128,128]{2,1,0:T(8,128)S(1)} %convolution_subtract_fusion, f32[128,128]{0,1:T(8,128)S(1)} %copy.169, f32[128,128]{0,1:T(8,128)S(1)} %copy.167), kind=kOutput, calls=%fused_computation.8 | convolution fusion | flops 605798400 | bytes 6422528 | tf_op jit(solution)/shard_map/ckq,jq->ckj/dot_general | solution.py:44
  106.4 3.3 copy.172
  109.6 3.2 reshape_reshape.14
  112.8 2.4 multiply_subtract_fusion.2
  115.9 1.9 fusion.42
  118.0 1.9 fusion.40
  120.0 1.9 fusion.5
  121.9 1.9 fusion.4
  123.9 2.0 fusion.18
  125.9 2.4 fusion.17
  128.3 2.0 fusion.2
  131.1 2.0 copy.188
  133.2 2.0 fusion.3
  136.3 0.9 fusion.9
  138.1 12.0 %copy.189 = f32[1,16384,4]{2,0,1:T(1,128)} copy(f32[1,16384,4]{1,2,0:T(4,128)S(1)} %get-tuple-element.17) | data formatting | bytes 524288 | tf_op jit(solution)/shard_map/transpose | solution.py:97
  150.7 74.4 %reduce = f32[16384,4]{1,0:T(8,128)} reduce(f32[16384,1,4]{2,1,0:T(1,128)} %bitcast.243, f32[]{:T(128)} %broadcast.236), dimensions={1}, to_apply=%bitcast.227.reduce_sub_computation | reduce | bytes 524292
  225.1 9.2 %reshape.147 = f32[32,1,2048]{2,1,0:T(1,128)} reshape(f32[16384,4]{1,0:T(8,128)} %reduce) | data formatting | bytes 524288
  234.3 6.0 %all-to-all-start.3 = ((f32[32,1,2048]{2,1,0:T(1,128)}), f32[32,1,2048]{2,1,0:T(1,128)S(1)}, u32[]{:S(2)}, u32[]{:S(2)}) async-start(f32[32,1,2048]{2,1,0:T(1,128)} %reshape.147), calls=%async_computation.3 | async-start | bytes 524288 | tf_op jit(solution)/shard_map/all_to_all | solution.py:100
  241.0 77.0 %all-reduce.3.cloned.1.call-done = f32[1,16384,4]{1,2,0:T(4,128)} async-done(((f32[1,16384,4]{1,2,0:T(4,128)}), f32[1,16384,4]{1,2,0:T(4,128)}) %all-reduce.3.cloned.1.call-update) | async-done | bytes 262160 | tf_op jit(solution)/shard_map/psum | solution.py:98
  318.0 14.8 %copy.192 = f32[1,16384,4]{2,0,1:T(1,128)} copy(f32[1,16384,4]{1,2,0:T(4,128)} %all-reduce.3.cloned.1.call-done) | data formatting | bytes 524288 | tf_op jit(solution)/shard_map/psum | solution.py:98
  332.8 74.4 %reduce.2 = f32[16384,4]{1,0:T(8,128)} reduce(f32[16384,1,4]{2,1,0:T(1,128)} %bitcast.244, f32[]{:T(128)} %broadcast.236), dimensions={1}, to_apply=%bitcast.229.reduce_sub_computation | reduce | bytes 524292
  407.3 9.1 %reshape.149 = f32[32,1,2048]{2,1,0:T(1,128)} reshape(f32[16384,4]{1,0:T(8,128)} %reduce.2) | data formatting | bytes 524288
  416.3 10.4 %all-to-all-start.4 = ((f32[32,1,2048]{2,1,0:T(1,128)}), f32[32,1,2048]{2,1,0:T(1,128)S(1)}, u32[]{:S(2)}, u32[]{:S(2)}) async-start(f32[32,1,2048]{2,1,0:T(1,128)} %reshape.149), calls=%async_computation.4 | async-start | bytes 524288 | tf_op jit(solution)/shard_map/all_to_all | solution.py:101
  426.8 1.2 reduce.1
  428.0 14.8 %reshape.148 = f32[16384,1,4]{2,1,0:T(1,128)} reshape(f32[32,2048]{1,0:T(8,128)S(1)} %reduce.1) | data formatting | bytes 524288
  442.8 5.3 %copy.212 = f32[1,32,512,4]{2,1,3,0:T(8,128)S(1)} copy(f32[1,32,512,4]{3,2,1,0:T(8,128)} %bitcast.245) | data formatting | bytes 524288 | tf_op jit(solution)/shard_map/all_to_all | solution.py:100
  449.7 1.2 reduce.3
  451.0 14.8 %reshape.150 = f32[16384,1,4]{2,1,0:T(1,128)} reshape(f32[32,2048]{1,0:T(8,128)S(1)} %reduce.3) | data formatting | bytes 524288
  465.7 15.0 %copy.193 = f32[1,16384,4]{1,2,0:T(4,128)S(1)} copy(f32[1,16384,4]{2,0,1:T(1,128)} %bitcast.246) | data formatting | bytes 524288 | tf_op jit(solution)/shard_map/all_to_all | solution.py:101
  (88 shorter events, 15.3 us)
Async XLA Ops:
  8.3 17.9 %copy-start.15 = (bf16[1,512,128]{2,1,0:T(8,128)(2,1)S(1)}, bf16[1,512,128]{2,1,0:T(8,128)(2,1)}, u32[]{:S(2)}) copy-start(bf16[1,512,128]{2,1,0:T(8,128)(2,1)} %param.8) | copy-start | bytes 393220
  9.4 16.9 %copy-start.16 = (bf16[1,512,128]{2,1,0:T(8,128)(2,1)S(1)}, bf16[1,512,128]{2,1,0:T(8,128)(2,1)}, u32[]{:S(2)}) copy-start(bf16[1,512,128]{2,1,0:T(8,128)(2,1)} %param.9) | copy-start | bytes 393220
  9.8 0.7 copy-start.5
  11.0 32.3 %copy-start.14 = (f32[512,128]{1,0:T(8,128)S(1)}, f32[512,128]{1,0:T(8,128)}, u32[]{:S(2)}) copy-start(f32[512,128]{1,0:T(8,128)} %param.10) | copy-start | bytes 786436
  11.9 26.5 %all-to-all-start = ((f32[32,1,512,4]{2,3,1,0:T(4,128)}), f32[32,1,512,4]{2,3,1,0:T(4,128)S(1)}, u32[]{:S(2)}, u32[]{:S(2)}) async-start(f32[32,1,512,4]{2,3,1,0:T(4,128)} %copy.153), calls=%async_computation | async-start | bytes 524288 | tf_op jit(solution)/shard_map/all_to_all | solution.py:59
  26.3 36.0 %copy-start.7 = (bf16[1,512,128]{1,0,2:T(2,128)(2,1)}, bf16[1,512,128]{1,0,2:T(2,128)(2,1)S(1)}, u32[]{:S(2)}) copy-start(bf16[1,512,128]{1,0,2:T(2,128)(2,1)S(1)} %copy.150) | copy-start | bytes 393220
  38.3 17.3 %all-to-all-start.2 = ((f32[1,512,128]{1,0,2:T(1,128)}), f32[1,512,128]{1,0,2:T(1,128)S(1)}, u32[]{:S(2)}, u32[]{:S(2)}) async-start(f32[1,512,128]{1,0,2:T(1,128)} %convert_multiply_fusion), calls=%async_computation.2 | async-start | bytes 524288 | tf_op jit(solution)/shard_map/all_to_all | solution.py:62
  55.6 18.1 %all-to-all-start.1 = ((f32[1,512,128]{1,0,2:T(1,128)}), f32[1,512,128]{1,0,2:T(1,128)S(1)}, u32[]{:S(2)}, u32[]{:S(2)}) async-start(f32[1,512,128]{1,0,2:T(1,128)} %copy.211), calls=%async_computation.1 | async-start | bytes 524288 | tf_op jit(solution)/shard_map/all_to_all | solution.py:63
  63.5 10.7 %copy-start.11 = (f32[16384]{0:T(1024)}, f32[16384]{0:T(1024)S(1)}, u32[]{:S(2)}) copy-start(f32[16384]{0:T(1024)S(1)} %fusion.52) | copy-start | bytes 196612
  65.0 9.9 %copy-start.1 = (f32[4,128,128]{1,2,0:T(8,128)}, f32[4,128,128]{1,2,0:T(8,128)S(1)}, u32[]{:S(2)}) copy-start(f32[4,128,128]{1,2,0:T(8,128)S(1)} %copy.165) | copy-start | bytes 786436
  74.1 0.7 copy-start.3
  79.4 2.9 copy-start.2
  79.4 2.8 copy-start.4
  109.6 3.2 copy-start
  121.9 1.9 copy-start.10
  135.3 1.0 copy-start.9
  135.3 1.0 copy-start.12
  135.3 1.0 copy-start.13
  234.3 182.0 %all-to-all-start.3 = ((f32[32,1,2048]{2,1,0:T(1,128)}), f32[32,1,2048]{2,1,0:T(1,128)S(1)}, u32[]{:S(2)}, u32[]{:S(2)}) async-start(f32[32,1,2048]{2,1,0:T(1,128)} %reshape.147), calls=%async_computation.3 | async-start | bytes 524288 | tf_op jit(solution)/shard_map/all_to_all | solution.py:100
  240.3 77.7 %all-reduce.3.cloned.1.call-start = ((), (), s32[]{:S(2)}) async-start(), calls=%async_computation.5 | async-start | bytes 524288 | tf_op jit(solution)/shard_map/psum | solution.py:98
  416.3 33.4 %all-to-all-start.4 = ((f32[32,1,2048]{2,1,0:T(1,128)}), f32[32,1,2048]{2,1,0:T(1,128)S(1)}, u32[]{:S(2)}, u32[]{:S(2)}) async-start(f32[32,1,2048]{2,1,0:T(1,128)} %reshape.149), calls=%async_computation.4 | async-start | bytes 524288 | tf_op jit(solution)/shard_map/all_to_all | solution.py:101
  442.8 5.6 %copy-start.6 = (f32[1,512,128]{1,0,2:T(1,128)S(1)}, f32[1,512,128]{1,0,2:T(1,128)}, u32[]{:S(2)}) copy-start(f32[1,512,128]{1,0,2:T(1,128)} %copy-done.5) | copy-start | bytes 786436
  442.8 5.6 %copy-start.8 = (bf16[1,512,128]{1,0,2:T(2,128)(2,1)S(1)}, bf16[1,512,128]{1,0,2:T(2,128)(2,1)}, u32[]{:S(2)}) copy-start(bf16[1,512,128]{1,0,2:T(2,128)(2,1)} %copy-done.7) | copy-start | bytes 393220
  442.8 5.6 %copy-start.17 = (f32[128]{0:T(128)S(1)}, f32[128]{0:T(128)}, u32[]{:S(2)}) copy-start(f32[128]{0:T(128)} %param.11) | copy-start | bytes 1540
Sparse Core Ops, SparseCore 0:
  244.3 73.6 all-reduce.2
